TPU v7x, 32 devices: a whole 2x2x4 slice. The times are simulated.
32 devices in a mesh: tower: 2 (over y), narrow: 4 (over z), wide: 4 (over x, core).
Axes of the slice: x: 2, y: 2, z: 4, core: 2. Of those that a mesh axis runs over, the one named last changes fastest.
Arguments:
- features: bfloat16 [4, 8, 256, 2048], P('narrow', ('tower', 'wide')), may hold values from -6 to 6
- w_in: bfloat16 [2048, 4096], P(None, 'narrow'), may hold values from -0.125 to 0.125
- b_in: float32 [4096], P('narrow'), may hold values from -0.5 to 0.5
- w_out: bfloat16 [4096, 256], P('narrow'), may hold values from -0.09375 to 0.09375
- user_emb: bfloat16 [8192, 256], P('narrow'), as said below
- item_ids: int32 [4, 8, 256], P('narrow', ('tower', 'wide')), may hold values from 0 to 8191
Outputs:
- row_loss: float32 [8192], P('narrow')
- item_grad: float32 [4, 8, 256, 256], P('narrow', ('tower', 'wide'))
Inputs may be any that keep to these rules, and one draw needn't show every extreme that they name: `user_emb`: user embeddings.
All inputs are finite; a program needn't handle non-finite values.
Results may differ from a plain program's by a relative error of at most 0.024.
Values may be sent and summed in bfloat16 or wider, within the bound.
A program may use at most 64 MiB of HBM per device.

v0:
```python
import jax
import jax.numpy as jnp
from jax import lax
from jax.sharding import PartitionSpec as P

INV_TEMP = 4.0
EPS = 1e-06
NEG = -1e30


def unit_rows(embed):
    return embed * lax.rsqrt(jnp.sum(embed * embed, axis=1, keepdims=True) + EPS)


def block_scores(user, rid, rglob, vectors, col_ids, col_glob):
    scores = (
        lax.dot_general(user, vectors, (((1,), (1,)), ((), ())), preferred_element_type=jnp.float32)
        * INV_TEMP
    )
    diag = rglob[:, None] == col_glob[None, :]
    keep = (rid[:, None] != col_ids[None, :]) | diag
    return (scores, diag, keep)


def block_scores_cols(vectors, col_ids, col_glob, user, rid, rglob):
    scores = (
        lax.dot_general(vectors, user, (((1,), (1,)), ((), ())), preferred_element_type=jnp.float32)
        * INV_TEMP
    )
    diag = col_glob[:, None] == rglob[None, :]
    keep = (col_ids[:, None] != rid[None, :]) | diag
    return (scores, diag, keep)


def local(features, w_in, b_in, w_out, user_emb, item_ids):
    share = features.shape[2]
    width = features.shape[3]
    embed_width = w_out.shape[1]
    users_dev = user_emb.shape[0]
    groups = lax.axis_size("narrow")
    panel = groups * share
    gathered, gathered_ids = (
        lax.all_gather(features, "narrow", axis=0, tiled=True),
        lax.all_gather(item_ids, "narrow", axis=0, tiled=True),
    )
    rows_in = gathered.reshape(panel, width)
    col_ids = gathered_ids.reshape(panel)
    hidden = jax.nn.relu(jnp.dot(rows_in, w_in, preferred_element_type=jnp.float32) + b_in).astype(
        jnp.bfloat16
    )
    partial_embed = jnp.dot(hidden, w_out, preferred_element_type=jnp.float32)
    item_vec = unit_rows(lax.psum(partial_embed, "narrow")).astype(jnp.bfloat16)
    row_ids = lax.all_gather(item_ids, ("tower", "wide"), axis=1, tiled=True).reshape(users_dev)
    narrow_index = lax.axis_index("narrow")
    panel_index = lax.axis_index(("tower", "wide"))
    row_glob = narrow_index * users_dev + jnp.arange(users_dev, dtype=jnp.int32)
    column = jnp.arange(panel, dtype=jnp.int32)
    col_glob = column // share * users_dev + panel_index * share + column % share
    block = min(512, users_dev)
    count = users_dev // block
    users = user_emb.reshape(count, block, embed_width)
    rid_blocks = row_ids.reshape(count, block)
    rglob_blocks = row_glob.reshape(count, block)

    def local_stats(blk):
        user, rid, rglob = blk
        scores, diag, keep = block_scores(user, rid, rglob, item_vec, col_ids, col_glob)
        masked = jnp.where(keep, scores, NEG)
        top = jnp.max(masked, axis=1)
        mass = jnp.sum(jnp.where(keep, jnp.exp(scores - top[:, None]), 0.0), axis=1)
        pos = jnp.sum(jnp.where(diag, scores, 0.0), axis=1)
        return (top, mass, pos, masked.T)

    def local_stats_only(blk):
        top, mass, pos, masked = local_stats(blk)
        return (top, mass, pos)

    top, mass, pos = lax.map(local_stats_only, (users, rid_blocks, rglob_blocks))
    top = top.reshape(users_dev)
    mass = mass.reshape(users_dev)
    pos = pos.reshape(users_dev)
    global_top = lax.pmax(top, ("tower", "wide"))
    total, global_pos = lax.psum((mass * jnp.exp(top - global_top), pos), ("tower", "wide"))
    lse = global_top + jnp.log(total)
    row_loss = lse - global_pos
    lse_blocks = lse.reshape(count, block)

    def add_block(acc, blk):
        user, rid, rglob, lse_blk = blk
        scores, diag, keep = block_scores_cols(item_vec, col_ids, col_glob, user, rid, rglob)
        coef = (
            jnp.where(keep, jnp.exp(scores - lse_blk[None, :]), 0.0) - diag.astype(jnp.float32)
        ).astype(jnp.bfloat16)
        term = jnp.dot(coef, user, preferred_element_type=jnp.float32)
        return (acc + term, None)

    acc, unused = lax.scan(
        add_block,
        jnp.zeros((share * lax.axis_size("narrow"), embed_width), jnp.float32),
        (users, rid_blocks, rglob_blocks, lse_blocks),
    )
    own_grad = lax.psum_scatter(INV_TEMP * acc, "narrow", scatter_dimension=0, tiled=True)
    return (row_loss, own_grad.reshape(1, 1, share, embed_width))


def solution(mesh):
    return jax.shard_map(
        local,
        mesh=mesh,
        in_specs=(
            P("narrow", ("tower", "wide"), None, None),
            P(None, "narrow"),
            P("narrow"),
            P("narrow", None),
            P("narrow", None),
            P("narrow", ("tower", "wide"), None),
        ),
        out_specs=(P("narrow"), P("narrow", ("tower", "wide"), None, None)),
        check_vma=False,
    )
```

profile of v0, /device:TPU:0, one launch (start us, length us, event | category | flops | bytes accessed | tf_op | source)
XLA Modules:
  0.0 238.5 jit_solution(5663523277225741020)
XLA Ops:
  7.2 0.0 copy-start
  7.2 0.0 all-gather.2.cloned.1.call-start
  7.2 0.7 all-gather.2.cloned.1.call-update
  7.9 0.0 all-reduce.3.cloned.1.call-start
  8.0 85.1 %all-gather.2.cloned.1.call-done = bf16[4,1,256,2048]{3,2,1,0:T(8,128)(2,1)} async-done(((bf16[1,1,256,2048]{3,2,1,0:T(8,128)(2,1)}), bf16[4,1,256,2048]{3,2,1,0:T(8,128)(2,1)}) %all-gather.2.cloned.1.call-update) | async-done | bytes 4194320 | tf_op jit(solution)/shard_map/all_gather | solution.py:43
  93.1 0.0 copy-done
  93.1 0.0 copy-start.1
  93.1 9.6 %fusion.48 = f32[1024,256]{1,0:T(8,128)} fusion(bf16[1024,256]{1,0:T(8,128)(2,1)S(1)} %copy-done, f32[1024]{0:T(1024)} %param.12, bf16[1024,2048]{1,0:T(8,128)(2,1)} %bitcast.95, bf16[2048,1024]{1,0:T(8,128)(2,1)} %param.11), kind=kOutput, calls=%fused_computation.64 | convolution fusion | flops 4834983936 | bytes 9965568 | tf_op jit(solution)/shard_map/dot_general | solution.py:51
  102.7 0.0 copy-start.2
  102.7 0.0 all-reduce.3.cloned.1.call-update
  102.7 0.0 reduce-scatter.2.cloned.1.call-start
  102.8 0.0 copy-done.1
  102.8 9.0 %all_gather.9 = s32[1,8,256]{2,0,1:T(1,128)S(1)} all-gather(s32[1,1,256]{2,0,1:T(1,128)S(1)} %bitcast.94), channel_id=1, replica_groups=mesh['tower'=2,'narrow'=4,'wide'=4] {'tower','wide'}, dimensions={1}, use_global_device_ids=true | all-gather | bytes 9216 | tf_op jit(solution)/shard_map/all_gather | solution.py:53
  111.9 8.8 %all_gather.10 = s32[4,1,256]{2,1,0:T(1,128)S(1)} all-gather(s32[1,1,256]{2,1,0:T(1,128)S(1)} %copy-done.1), channel_id=1, replica_groups=mesh['tower'=2,'narrow'=4,'wide'=4] {'narrow'}, dimensions={0}, use_global_device_ids=true | all-gather | bytes 5120 | tf_op jit(solution)/shard_map/all_gather | solution.py:44
  120.7 32.6 %all-reduce.3.cloned.1.call-done = f32[1024,256]{1,0:T(8,128)} async-done(((f32[1024,256]{1,0:T(8,128)}), f32[1024,256]{1,0:T(8,128)}) %all-reduce.3.cloned.1.call-update) | async-done | bytes 1048592 | tf_op jit(solution)/shard_map/psum | solution.py:52
  153.3 1.4 multiply_reduce_fusion
  154.8 1.4 multiply_convert_fusion
  156.2 0.0 copy-done.2
  156.2 7.8 %while.26 = (s32[]{:T(128)}, f32[4,512]{1,0:T(4,128)S(1)}, f32[4,512]{1,0:T(4,128)S(1)}, f32[4,512]{1,0:T(4,128)S(1)}, s32[4,512]{1,0:T(4,128)S(1)}, /*index=5*/...) while((s32[]{:T(128)}, f32[4,512]{1,0:T(4,128)S(1)}, ...), condition=%wide.region_6.7_spmd.clone, body=%wide.region_2.6_spmd.clone.sunk | while | flops 276313600 | bytes 5038221 | solution.py:78
  156.2 0.7 select_reduce_fusion.3
  156.9 1.1 fusion.70
  158.0 0.1 dynamic_update_slice.17
  158.1 0.1 dynamic_update_slice.16
  158.2 0.7 select_reduce_fusion.3
  158.9 1.1 fusion.70
  160.0 0.1 dynamic_update_slice.17
  160.0 0.1 dynamic_update_slice.16
  160.1 0.7 select_reduce_fusion.3
  160.8 1.1 fusion.70
  162.0 0.1 dynamic_update_slice.17
  162.0 0.1 dynamic_update_slice.16
  162.1 0.7 select_reduce_fusion.3
  162.8 1.1 fusion.70
  163.9 0.1 dynamic_update_slice.17
  164.0 0.1 dynamic_update_slice.16
  164.0 14.1 %pmax.7 = f32[2048]{0:T(1024)S(1)} all-reduce(f32[2048]{0:T(1024)S(1)} %bitcast.84), channel_id=1, replica_groups=mesh['tower'=2,'narrow'=4,'wide'=4] {'tower','wide'}, use_global_device_ids=true, to_apply=%region_7.8 | all-reduce | flops 2048 | bytes 16384 | tf_op jit(solution)/shard_map/pmax | solution.py:82
  178.2 22.3 %all-reduce = (f32[2048]{0:T(1024)S(1)}, f32[2048]{0:T(1024)S(1)}) all-reduce(f32[2048]{0:T(1024)S(1)} %exponential_multiply_fusion, f32[2048]{0:T(1024)S(1)} %bitcast.89), channel_id=1, replica_groups=mesh['tower'=2,'narrow'=4,'wide'=4] {'tower','wide'}, use_global_device_ids=true, to_apply=%region_8.9 | all-reduce | flops 4096 | bytes 32768 | tf_op jit(solution)/shard_map/psum | solution.py:83
  200.5 0.6 fusion.54
  201.1 4.9 %while.27 = (s32[]{:T(128)}, f32[1024,256]{1,0:T(8,128)S(1)}, s32[4,1,256]{2,1,0:T(1,128)S(1)}, s32[4,512]{1,0:T(4,128)S(1)}, s32[4,512]{1,0:T(4,128)S(1)}, /*in...) while((s32[]{:T(128)}, f32[1024,256]{1,0:T(8,128)S(1)}, ...), condition=%wide.region_11.12_spmd.clone, body=%wide.region_10.11_spmd.clone.sunk | while | flops 542129152 | bytes 3177603 | solution.py:97
  201.2 1.2 fusion.75
  202.4 1.2 fusion.75
  203.7 1.2 fusion.75
  204.9 1.2 fusion.75
  206.1 1.1 broadcast_multiply_fusion
  207.1 0.0 reduce-scatter.2.cloned.1.call-update
  207.2 24.8 %reduce-scatter.2.cloned.1.call-done = f32[256,256]{1,0:T(8,128)} async-done(((f32[1024,256]{1,0:T(8,128)}), f32[256,256]{1,0:T(8,128)}) %reduce-scatter.2.cloned.1.call-update) | async-done | bytes 262160 | tf_op jit(solution)/shard_map/reduce_scatter | solution.py:102
  (37 shorter events, 0.5 us)
Async XLA Ops:
  7.2 85.9 %copy-start = (bf16[1024,256]{1,0:T(8,128)(2,1)S(1)}, bf16[1024,256]{1,0:T(8,128)(2,1)}, u32[]{:S(2)}) copy-start(bf16[1024,256]{1,0:T(8,128)(2,1)} %param.13) | copy-start | bytes 1572868
  7.2 85.9 %all-gather.2.cloned.1.call-start = ((), (), s32[]{:S(2)}) async-start(), calls=%async_computation.1 | async-start | bytes 5242880 | tf_op jit(solution)/shard_map/all_gather | solution.py:43
  7.9 145.4 %all-reduce.3.cloned.1.call-start = ((), (), s32[]{:S(2)}) async-start(), calls=%async_computation.2 | async-start | bytes 2097152 | tf_op jit(solution)/shard_map/psum | solution.py:52
  93.1 9.8 %copy-start.1 = (s32[1,1,256]{2,1,0:T(1,128)S(1)}, s32[1,1,256]{2,1,0:T(1,128)}, u32[]{:S(2)}) copy-start(s32[1,1,256]{2,1,0:T(1,128)} %param.15) | copy-start | bytes 3076
  102.7 53.5 %copy-start.2 = (bf16[2048,256]{1,0:T(8,128)(2,1)S(1)}, bf16[2048,256]{1,0:T(8,128)(2,1)}, u32[]{:S(2)}) copy-start(bf16[2048,256]{1,0:T(8,128)(2,1)} %param.14) | copy-start | bytes 3145732
  102.7 129.3 %reduce-scatter.2.cloned.1.call-start = ((), (), s32[]{:S(2)}) async-start(), calls=%async_computation.3 | async-start | bytes 1310720 | tf_op jit(solution)/shard_map/reduce_scatter | solution.py:102
Sparse Core Ops, SparseCore 0:
  9.6 83.4 all-gather.1
  102.9 50.3 all-reduce.2
  207.3 24.6 reduce-scatter.1
where the time goes:
time: 239 us
  waiting for transfers between devices  143 us (60%)
  blocking collectives  54.2 us (23%)
  matrix products  17 us (7%)
  between operations  13.9 us (6%)
  other arithmetic  8.95 us (4%)
    all_gather x1, waiting for transfers between devices, local(): lax.all_gather(features, 'narrow', axis=0, tiled=True)  85.1 us
    psum x1, waiting for transfers between devices, local(): item_vec = unit_rows(lax.psum(partial_embed, 'narrow')).astype(jnp.bfloat16)  32.6 us
    reduce_scatter x1, waiting for transfers between devices, local(): lax.psum_scatter(INV_TEMP * acc, 'narrow', scatter_dimension=0, tiled=True)  24.8 us
    psum x1, blocking collectives, local(): lax.psum((mass * jnp.exp(top - global_top), pos), ('tower', 'wide'))  22.3 us
    pmax x1, blocking collectives, local(): global_top = lax.pmax(top, ('tower', 'wide'))  14.1 us
    dot_general x1, matrix products, local(): partial_embed = jnp.dot(hidden, w_out, preferred_element_type=jnp.float32)  9.62 us
    all_gather x1, blocking collectives, local(): lax.all_gather(item_ids, ('tower', 'wide'), axis=1, tiled=True)  9.02 us
    all_gather x1, blocking collectives, local(): lax.all_gather(item_ids, 'narrow', axis=0, tiled=True)  8.76 us
  transfers between devices with their start and end apart: 3, of which 3 were waited for; matrix products, arithmetic and copies ran while one was open for 0% of the time, Pallas kernels for 0%

commit v1 on v0

--- a/solution.py
+++ b/solution.py
@@ -1,6 +1,8 @@
 import jax
 import jax.numpy as jnp
 from jax import lax
+from jax.experimental import pallas as pl
+from jax.experimental.pallas import tpu as pltpu
 from jax.sharding import PartitionSpec as P
 
 INV_TEMP = 4.0
@@ -103,9 +105,394 @@
     return (row_loss, own_grad.reshape(1, 1, share, embed_width))
 
 
+MESH = pl.DeviceIdType.MESH
+LOW = -1e20
+ROW_PARTS = 2
+PARTS = ROW_PARTS + 2
+
+
+def coords(k):
+    return {"narrow": k // 8, "tower": (k // 4) % 2, "wide": k % 4}
+
+
+def fused(
+    feat_ref, w_in_ref, b_in_ref, w_out_ref, users_ref, ids_ref, ids_col_ref,
+    loss_ref, grad_ref,
+    xg, wg, wog, bg, ug, idg, acc, core_in, y_out, y_in, vec, held, stats, stats_in, fin, fin_in,
+    local_sem, fy_send, fy_recv, fc_send, fc_recv, wz_send, wz_recv, wx_send, wx_recv,
+    uz_send, uz_recv, ux_send, ux_recv, uy_send, uy_recv, uc_send, uc_recv,
+    rs_sem, small_send, small_recv,
+):
+    z = lax.axis_index("narrow")
+    t = lax.axis_index("tower")
+    wide = lax.axis_index("wide")
+    x, c = wide // 2, wide % 2
+    p = t * 4 + wide
+    me = z * 8 + p
+    ox, oc, ot = 1 - x, 1 - c, 1 - t
+    xdev = {"wide": ox * 2 + c}
+    cdev = {"wide": x * 2 + oc}
+    ydev = {"tower": ot}
+    share = feat_ref.shape[0]
+    rows = wg.shape[2] // ROW_PARTS
+
+    def peer(i):
+        return lax.rem(me + i, 32)
+
+    barrier = pltpu.get_barrier_semaphore()
+
+    @pl.loop(1, 32)
+    def _(i):
+        pl.semaphore_signal(barrier, inc=1, device_id=coords(peer(i)), device_id_type=MESH)
+
+    local = []
+
+    def bring(src, dst):
+        copy = pltpu.make_async_copy(src, dst, local_sem.at[len(local)])
+        copy.start()
+        local.append(copy)
+
+    for i in range(2):
+        unit = t * 4 + i * 2 + c
+        bring(w_in_ref.at[:, pl.ds(pl.multiple_of(unit * 128, 128), 128)], wg.at[z, i])
+        bring(w_out_ref.at[unit], wog.at[z, i])
+        bring(b_in_ref.at[unit], bg.at[z, i])
+    bring(feat_ref, xg.at[c * 2 + t])
+    bring(users_ref, ug.at[pl.ds(z * 8, 8)])
+    bring(ids_ref, idg.at[me])
+
+    pl.semaphore_wait(barrier, 31)
+
+    def remote(src, dst, send, recv, dev):
+        return pltpu.make_async_remote_copy(
+            src_ref=src, dst_ref=dst, send_sem=send, recv_sem=recv, device_id=dev, device_id_type=MESH
+        )
+
+    sent = []
+
+    def send(make):
+        make().start()
+        sent.append(make)
+
+    own = c * 2 + t
+    send(lambda: remote(feat_ref, xg.at[own], fy_send, fy_recv, ydev))
+    send(lambda: remote(feat_ref, xg.at[own], fc_send.at[0], fc_recv.at[0], cdev))
+
+    for copy in local[:6]:
+        copy.wait()
+
+    def part(b, i, ch):
+        if ch < ROW_PARTS:
+            return wg.at[b, i, pl.ds(ch * rows, rows)]
+        return wog.at[b, i] if ch == ROW_PARTS else bg.at[b, i]
+
+    def z_copy(b, ch, to):
+        return remote(
+            part(b, x, ch), part(b, x, ch), wz_send.at[to - z + 1, b, ch], wz_recv.at[b, ch], {"narrow": to}
+        )
+
+    def x_copy(b, i, ch):
+        return remote(part(b, i, ch), part(b, i, ch), wx_send.at[b, ch], wx_recv.at[b, ch], xdev)
+
+    zsends = []
+
+    def z_send(make, cond, ):
+        pl.when(cond)(lambda: make().start())
+        zsends.append((make, cond))
+
+    order = [PARTS - 2, PARTS - 1] + list(range(ROW_PARTS))
+    for ch in order:
+        for to, cond in ((z - 1, z > 0), (z + 1, z < 3)):
+            z_send(lambda ch=ch, to=to: z_copy(z, ch, to), cond)
+
+    blocks = [1 + z % 2, (2 + 3 * z) % 5, 3 * (1 - z // 2)]
+    onward = [jnp.where(b > z, z - 1, z + 1) for b in blocks]
+    goes = [(to >= 0) & (to <= 3) for to in onward]
+
+    def ids_copy(k):
+        return remote(idg.at[me], idg.at[me], small_send.at[0], small_recv.at[0], coords(k))
+
+    for copy in local[6:]:
+        copy.wait()
+
+    @pl.loop(1, 32)
+    def _(i):
+        ids_copy(peer(i)).start()
+
+    def forward(j, z_part=True, mid=None):
+        b, to, go = blocks[j], onward[j], goes[j]
+        for ch in order:
+            make = lambda ch=ch: z_copy(b, ch, to)
+            x_copy_make = lambda ch=ch: x_copy(b, x, ch)
+            z_copy(b, ch, z).wait_recv()
+            pl.when(go)(lambda: make().start())
+            x_copy_make().start()
+
+    def forward_done(j):
+        b, to, go = blocks[j], onward[j], goes[j]
+        for ch in order:
+            pl.when(go)(lambda: z_copy(b, ch, to).wait_send())
+            x_copy(b, x, ch).wait_send()
+
+    def x_arrived(j):
+        for ch in order:
+            x_copy(blocks[j], ox, ch).wait_recv()
+
+    def compute(b, first=False):
+        @pl.loop(0, 4)
+        def _(s):
+            weights = jnp.concatenate([wg[b, 0], wg[b, 1]], axis=1)
+            bias = jnp.concatenate([bg[b, 0], bg[b, 1]], axis=1)
+            outer = jnp.concatenate([wog[b, 0], wog[b, 1]], axis=0)
+            h = jnp.dot(xg[s], weights, preferred_element_type=jnp.float32) + bias
+            h = jnp.maximum(h, 0.0).astype(jnp.bfloat16)
+            e = jnp.dot(h, outer, preferred_element_type=jnp.float32)
+            acc[s] = e if first else acc[s] + e
+
+    forward(0)
+    forward(1)
+
+    def u_z(n, to):
+        k = n * 8 + p
+        return remote(ug.at[k], ug.at[k], uz_send.at[to - z + 1, n], uz_recv.at[n], {"narrow": to})
+
+    def slot(i, j):
+        return (t + i - 2 * t * i) * 4 + (x + j - 2 * x * j) * 2 + c
+
+    def u_x(n, j):
+        k = n * 8 + slot(0, j)
+        return remote(ug.at[k], ug.at[k], ux_send.at[n], ux_recv.at[n], xdev)
+
+    def u_y(n, i, j):
+        k = n * 8 + slot(i, j)
+        return remote(ug.at[k], ug.at[k], uy_send.at[n, j], uy_recv.at[n, j], ydev)
+
+    def u_c(n, i, j, lane):
+        k = n * 8 + slot(i, j) - c + lane
+        return remote(ug.at[k], ug.at[k], uc_send.at[n, i, j], uc_recv.at[n, i, j], cdev)
+
+    for to, cond in ((z - 1, z > 0), (z + 1, z < 3)):
+        z_send(lambda to=to: u_z(z, to), cond)
+
+    def u_forward(j):
+        n, to, go = blocks[j], onward[j], goes[j]
+        u_z(n, z).wait_recv()
+        z_send(lambda: u_z(n, to), go)
+        send(lambda: u_x(n, 0))
+        send(lambda: u_y(n, 0, 0))
+        send(lambda: u_c(n, 0, 0, c))
+
+    def u_cross(j):
+        n = blocks[j]
+        u_x(n, 1).wait_recv()
+        send(lambda: u_y(n, 0, 1))
+        send(lambda: u_c(n, 0, 1, c))
+
+    def u_over(j):
+        n = blocks[j]
+        for k in range(2):
+            u_y(n, 1, k).wait_recv()
+            send(lambda k=k: u_c(n, 1, k, c))
+
+    def u_ready(j):
+        n = blocks[j]
+        for i in range(2):
+            for k in range(2):
+                u_c(n, i, k, oc).wait_recv()
+
+    middle = (z > 0) & (z < 3)
+    edge = (z == 0) | (z == 3)
+    pl.when(middle)(lambda: forward(2))
+
+    y_slot = c * 2 + ot
+    remote(xg.at[y_slot], xg.at[y_slot], fy_send, fy_recv, ydev).wait_recv()
+    send(lambda: remote(xg.at[y_slot], xg.at[y_slot], fc_send.at[1], fc_recv.at[1], cdev))
+    for i, other in enumerate((oc * 2 + t, oc * 2 + ot)):
+        remote(xg.at[other], xg.at[other], fc_send.at[i], fc_recv.at[i], cdev).wait_recv()
+
+    compute(z, first=True)
+    x_arrived(0)
+    compute(blocks[0])
+    x_arrived(1)
+    compute(blocks[1])
+    pl.when(edge)(lambda: forward(2))
+    u_forward(0)
+    x_arrived(2)
+    compute(blocks[2])
+
+    core_copy = lambda: remote(acc.at[pl.ds(oc * 2, 2)], core_in, rs_sem.at[0], rs_sem.at[1], cdev)
+    send(core_copy)
+    u_forward(1)
+    u_cross(0)
+    core_copy().wait_recv()
+    y_out[...] = acc[c * 2 + ot] + core_in[ot]
+    y_copy = lambda: remote(y_out, y_in, rs_sem.at[2], rs_sem.at[3], ydev)
+    send(y_copy)
+    u_forward(2)
+    u_cross(1)
+    u_over(0)
+    y_copy().wait_recv()
+    embed = acc[own] + core_in[t] + y_in[...]
+    norm = lax.rsqrt(jnp.sum(embed * embed, axis=1, keepdims=True) + EPS)
+    vec[...] = (embed * norm).astype(jnp.bfloat16)
+
+    def ids_all():
+        ref = idg.at[pl.ds(0, 31)]
+        return pltpu.make_async_copy(ref, ref, small_recv.at[0])
+
+    ids_all().wait()
+    spread = lax.broadcasted_iota(jnp.int32, (share, share), 0) - lax.broadcasted_iota(
+        jnp.int32, (share, share), 1
+    )
+
+    def raw(k):
+        s = lax.dot_general(vec[...], ug[k], (((1,), (1,)), ((), ())), preferred_element_type=jnp.float32)
+        return s * INV_TEMP
+
+    def score(k):
+        s = raw(k)
+        keep = (ids_col_ref[...] != idg[k]) | (spread == (k - me) * 512)
+        s = jnp.where(keep, s, NEG)
+        top = jnp.maximum(jnp.max(s, axis=0, keepdims=True), LOW)
+        e = jnp.exp(s - top)
+        held[k] = e
+        stats[k, 0:1] = top
+        stats[k, 1:2] = jnp.sum(e, axis=0, keepdims=True)
+
+    def score_block(n):
+        @pl.loop(0, 4)
+        def _(i):
+            for half in range(2):
+                score(n * 8 + i * 2 + half)
+
+    score_block(z)
+    fin[1:2] = jnp.sum(jnp.where(spread == 0, raw(me), 0.0), axis=0, keepdims=True)
+    u_cross(2)
+    u_over(1)
+    u_over(2)
+    for j in range(3):
+        u_ready(j)
+        score_block(blocks[j])
+
+    def stats_copy(k):
+        return remote(stats.at[k], stats_in.at[me], small_send.at[1], small_recv.at[1], coords(k))
+
+    @pl.loop(1, 32)
+    def _(i):
+        stats_copy(peer(i)).start()
+
+    stats_in[me] = stats[me]
+    ref_in = stats_in.at[pl.ds(0, 31)]
+    pltpu.make_async_copy(ref_in, ref_in, small_recv.at[1]).wait()
+    got = stats_in[...]
+    tops, sums = got[:, 0, :], got[:, 1, :]
+    top = jnp.max(tops, axis=0, keepdims=True)
+    total = jnp.sum(sums * jnp.exp(tops - top), axis=0, keepdims=True)
+    lse = top + jnp.log(total)
+    fin[0:1] = lse
+    fin[1:2] = lse - fin[1:2]
+    fin_in[me] = fin[...]
+
+    def fin_copy(k):
+        return remote(fin, fin_in.at[me], small_send.at[2], small_recv.at[2], coords(k))
+
+    @pl.loop(1, 32)
+    def _(i):
+        fin_copy(peer(i)).start()
+
+    ref_fin = fin_in.at[pl.ds(0, 31)]
+    pltpu.make_async_copy(ref_fin, ref_fin, small_recv.at[2]).wait()
+
+    grad_ref[...] = -ug[me].astype(jnp.float32)
+
+    @pl.loop(0, 8)
+    def _(i):
+        coefs, users = [], []
+        for q in range(4):
+            k = i * 4 + q
+            factor = jnp.exp(stats[k, 0:1] - fin_in[k, 0:1])
+            coefs.append((held[k] * factor).astype(jnp.bfloat16))
+            users.append(ug[k])
+        grad_ref[...] += jnp.dot(
+            jnp.concatenate(coefs, axis=1), jnp.concatenate(users, axis=0), preferred_element_type=jnp.float32
+        )
+
+    grad_ref[...] = grad_ref[...] * INV_TEMP
+    loss_ref[...] = fin_in[pl.ds(z * 8, 8), 1, :]
+
+    for make in sent:
+        make().wait_send()
+    for make, cond in zsends:
+        pl.when(cond)(lambda make=make: make().wait_send())
+    for j in range(3):
+        forward_done(j)
+    for buf, sem in ((idg, 0), (stats_in, 1), (fin_in, 2)):
+        ref = buf.at[pl.ds(0, 31)]
+        pltpu.make_async_copy(ref, ref, small_send.at[sem]).wait()
+
+
+def local_fused(features, w_in, b_in, w_out, user_emb, item_ids):
+    share, width = features.shape[2:]
+    embed = w_out.shape[1]
+    f32, bf16, i32 = jnp.float32, jnp.bfloat16, jnp.int32
+    hbm = pl.BlockSpec(memory_space=pl.ANY)
+    vmem = pl.BlockSpec(memory_space=pltpu.VMEM)
+    dma = pltpu.SemaphoreType.DMA
+    row_loss, grad = pl.pallas_call(
+        fused,
+        out_shape=(
+            jax.ShapeDtypeStruct((8, share), f32),
+            jax.ShapeDtypeStruct((share, embed), f32),
+        ),
+        in_specs=[hbm, hbm, hbm, hbm, hbm, hbm, vmem],
+        out_specs=(vmem, vmem),
+        scratch_shapes=[
+            pltpu.VMEM((4, share, width), bf16),
+            pltpu.VMEM((4, 2, width, 128), bf16),
+            pltpu.VMEM((4, 2, 128, embed), bf16),
+            pltpu.VMEM((4, 2, 1, 128), f32),
+            pltpu.VMEM((32, share, embed), bf16),
+            pltpu.VMEM((32, 1, share), i32),
+            pltpu.VMEM((4, share, embed), f32),
+            pltpu.VMEM((2, share, embed), f32),
+            pltpu.VMEM((share, embed), f32),
+            pltpu.VMEM((share, embed), f32),
+            pltpu.VMEM((share, embed), bf16),
+            pltpu.VMEM((32, share, share), f32),
+            pltpu.VMEM((32, 2, share), f32),
+            pltpu.VMEM((32, 2, share), f32),
+            pltpu.VMEM((2, share), f32),
+            pltpu.VMEM((32, 2, share), f32),
+            dma((9,)),
+            dma, dma, dma((2,)), dma((2,)),
+            dma((3, 4, PARTS)), dma((4, PARTS)), dma((4, PARTS)), dma((4, PARTS)),
+            dma((3, 4)), dma((4,)), dma((4,)), dma((4,)),
+            dma((4, 2)), dma((4, 2)), dma((4, 2, 2)), dma((4, 2, 2)),
+            dma((4,)), dma((3,)), dma((3,)),
+        ],
+        compiler_params=pltpu.CompilerParams(
+            collective_id=0, has_side_effects=True, vmem_limit_bytes=44 * 1024 * 1024
+        ),
+        cost_estimate=pl.CostEstimate(flops=8 * 10**9, bytes_accessed=4 * 10**6, transcendentals=2 * 10**6),
+    )(
+        features.reshape(share, width),
+        w_in,
+        b_in.reshape(8, 1, 128),
+        w_out.reshape(8, 128, embed),
+        user_emb.reshape(8, share, embed),
+        item_ids.reshape(1, share),
+        item_ids.reshape(share, 1),
+    )
+    return row_loss.reshape(8 * share), grad.reshape(1, 1, share, embed)
+
+
+def fits(mesh):
+    return dict(mesh.shape) == {"tower": 2, "narrow": 4, "wide": 4}
+
+
 def solution(mesh):
     return jax.shard_map(
-        local,
+        local_fused if fits(mesh) else local,
         mesh=mesh,
         in_specs=(
             P("narrow", ("tower", "wide"), None, None),

time: 239 us -> 111 us (0.46)
  waiting for transfers between devices: 143 us -> 0 us
  Pallas kernels: 0 us -> 101 us
  blocking collectives: 54.2 us -> 0 us
  matrix products: 17 us -> 0 us
  between operations: 13.9 us -> 0.66 us
  other arithmetic: 8.95 us -> 0 us
  local copies, waits for them, and re-layouts: 0.76 us -> 9.15 us
    pallas_call x0 -> x1, Pallas kernels: none -> 101 us  [local_fused(): pl.pallas_call(fused, out_shape=(jax.ShapeDtypeStruct((8, share), f32), j...]
    all_gather x1 -> x0, waiting for transfers between devices: 85.1 us -> none  [local(): lax.all_gather(features, 'narrow', axis=0, tiled=True)]
    psum x1 -> x0, waiting for transfers between devices: 32.6 us -> none  [local(): item_vec = unit_rows(lax.psum(partial_embed, 'narrow')).astype(jnp.bfloat16)]
    reduce_scatter x1 -> x0, waiting for transfers between devices: 24.8 us -> none  [local(): lax.psum_scatter(INV_TEMP * acc, 'narrow', scatter_dimension=0, tiled=True)]
    psum x1 -> x0, blocking collectives: 22.3 us -> none  [local(): lax.psum((mass * jnp.exp(top - global_top), pos), ('tower', 'wide'))]
    all_gather x2 -> x0, blocking collectives: 17.8 us -> none  [the longest x1 9.02 us: local(): lax.all_gather(item_ids, ('tower', 'wide'), axis=1, tiled=True)]
    dot_general x9 -> x0, matrix products: 17 us -> none  [the longest x1 9.62 us: local(): partial_embed = jnp.dot(hidden, w_out, preferred_element_type=jnp.float32)]
    pmax x1 -> x0, blocking collectives: 14.1 us -> none  [local(): global_top = lax.pmax(top, ('tower', 'wide'))]
  transfers between devices with their start and end apart: 3 -> 0, of which waited for: 3 -> 0; matrix products, arithmetic and copies ran while one was open for 0% -> 0% of each run, Pallas kernels for 0% -> 0%
where the time goes in v1:
time: 111 us
  Pallas kernels  101 us (91%)
  local copies, waits for them, and re-layouts  9.15 us (8%)
    pallas_call x1, Pallas kernels, local_fused(): pl.pallas_call(fused, out_shape=(jax.ShapeDtypeStruct((8, share), f32), j...  101 us
    unnamed x14, local copies, waits for them, and re-layouts  8.35 us

profile of v1, /device:TPU:0, one launch (start us, length us, event | category | flops | bytes accessed | tf_op | source)
XLA Modules:
  0.0 111.0 jit_solution(13841046775897538394)
XLA Ops:
  0.6 0.8 copy.8.ids_col_ref
  1.4 0.0 copy-start
  1.5 0.7 copy-done
  2.1 0.0 copy-start.1
  2.1 2.2 %copy-done.1 = bf16[2048,1024]{1,0:T(8,128)(2,1)S(1)} copy-done((bf16[2048,1024]{1,0:T(8,128)(2,1)S(1)}, bf16[2048,1024]{1,0:T(8,128)(2,1)}, u32[]{:S(2)}) %copy-start.1) | copy-done | bytes 4194328
  4.3 0.0 copy-start.2
  4.3 1.2 %copy-done.2 = bf16[1,1,256,2048]{3,2,1,0:T(8,128)(2,1)S(1)} copy-done((bf16[1,1,256,2048]{3,2,1,0:T(8,128)(2,1)S(1)}, bf16[1,1,256,2048]{3,2,1,0:T(8,128)(2,1)}, u32[]{:S(2)}) %copy-start.2) | copy-done | bytes 1048600
  5.5 0.0 copy-start.3
  5.5 1.2 %copy-done.3 = bf16[2048,256]{1,0:T(8,128)(2,1)S(1)} copy-done((bf16[2048,256]{1,0:T(8,128)(2,1)S(1)}, bf16[2048,256]{1,0:T(8,128)(2,1)}, u32[]{:S(2)}) %copy-start.3) | copy-done | bytes 1048600
  6.8 0.0 copy-start.4
  6.8 1.0 copy-done.4
  7.8 0.0 copy-start.5
  7.8 0.7 copy-done.5
  8.5 101.1 %shard_map.77 = (f32[8,256]{1,0:T(8,128)S(1)}, f32[256,256]{1,0:T(8,128)S(1)}) custom-call(bf16[256,2048]{1,0:T(8,128)(2,1)S(1)} %bitcast.13, bf16[2048,1024]{1,0:T(8,128)(2,1)S(1)} %copy-done.1, f32[8,1,128]{2,1,0:T(1,128)S(1)} %bitcast.16, bf16[8,128,256]{2,1,0:T(8,128)(2,1)S(1)} %bitcast.15, bf16[8,256,256]{2,1,0:T(8,128)(2,1)S(1)} %bitcast.14, ...), custom_call_target="tpu_custom_call" | custom-call | flops 8000000000 | bytes 4000000 | tf_op jit(solution)/shard_map/pallas_call | solution.py:441
  109.6 0.6 copy.9
  110.2 0.7 copy.11
Async XLA Ops:
  1.4 0.7 copy-start
  2.1 2.2 %copy-start.1 = (bf16[2048,1024]{1,0:T(8,128)(2,1)S(1)}, bf16[2048,1024]{1,0:T(8,128)(2,1)}, u32[]{:S(2)}) copy-start(bf16[2048,1024]{1,0:T(8,128)(2,1)} %w_in_ref.1) | copy-start | bytes 12582916
  4.3 1.2 %copy-start.2 = (bf16[1,1,256,2048]{3,2,1,0:T(8,128)(2,1)S(1)}, bf16[1,1,256,2048]{3,2,1,0:T(8,128)(2,1)}, u32[]{:S(2)}) copy-start(bf16[1,1,256,2048]{3,2,1,0:T(8,128)(2,1)} %param.6) | copy-start | bytes 3145732
  5.5 1.2 %copy-start.3 = (bf16[2048,256]{1,0:T(8,128)(2,1)S(1)}, bf16[2048,256]{1,0:T(8,128)(2,1)}, u32[]{:S(2)}) copy-start(bf16[2048,256]{1,0:T(8,128)(2,1)} %param.10) | copy-start | bytes 3145732
  6.8 1.0 copy-start.4
  7.8 0.7 copy-start.5
